TPU v7x, 32 devices: a whole 2x2x4 slice. The times are simulated.
32 devices in a mesh: depth: 4 (over z), row: 2 (over core), col: 4 (over y, x).
Axes of the slice: x: 2, y: 2, z: 4, core: 2. Of those that a mesh axis runs over, the one named last changes fastest.
Arguments:
- linv_root: float32 [4096, 4096], P(('depth', 'row'))
- child_factor: float32 [4, 4096, 2048], P('depth', 'col', 'row'), may hold values from -0.125 to 0.125
- child_inverse: float32 [4, 2048, 2048], P('depth', 'col')
- structure: int32 [4, 32], P('depth', 'col'), may hold values 0 or 1
Outputs:
- sigma_root: float32 [4096, 4096], P(('depth', 'row'), 'col')
- sigma_cross: float32 [4, 4096, 2048], P('depth', 'col', 'row')
- sigma_child: float32 [4, 2048, 2048], P('depth', 'col', 'row')
All inputs are finite; a program needn't handle non-finite values. No bound on the sum of `structure` on one device may be relied on, other than what follows from the above.
Results may differ from a plain program's by a relative error of at most 0.00015.
Values sent between devices are 32-bit elements; how exact they have to be, the bound alone decides.
A program may use at most 192 MiB of HBM per device.

v0:
```python
import jax
import jax.numpy as jnp
from jax import lax
from jax.sharding import PartitionSpec as P

TILE = 128


def contract_rows(left, right):
    return lax.dot_general(
        left,
        right,
        (((0,), (0,)), ((), ())),
        precision=lax.Precision.HIGHEST,
        preferred_element_type=jnp.float32,
    )


def shards(linv_root, child_factor, child_inverse, structure):
    highest = lax.Precision.HIGHEST
    n_col = lax.axis_size("col")
    n_row = lax.axis_size("row")
    col_at = lax.axis_index("col")
    row_at = lax.axis_index("row")
    root_rows = linv_root.shape[0]
    col_width = linv_root.shape[1] // n_col
    flat_at = lax.axis_index("depth") * n_row + row_at
    root_cols = lax.dynamic_slice_in_dim(linv_root, col_at * col_width, col_width, 1)
    term_value = contract_rows(linv_root, root_cols)
    column_panel = lax.psum(term_value, ("depth", "row"))
    sigma_root = lax.dynamic_slice_in_dim(column_panel, flat_at * root_rows, root_rows, 0)
    factor = child_factor[0]
    inverse = child_inverse[0]
    tile_mask = jnp.repeat(structure[0], TILE).astype(jnp.float32)[:, None]
    masked_factor = factor * tile_mask
    factor_panel = lax.all_gather(masked_factor, "row", axis=1, tiled=True)
    nj_row = factor.shape[1]
    inverse_block = lax.dynamic_slice_in_dim(inverse, row_at * nj_row, nj_row, 1)
    update = jnp.dot(
        factor_panel,
        lax.all_gather(inverse_block, "col", axis=0, tiled=True),
        precision=highest,
        preferred_element_type=jnp.float32,
    )
    weighted = contract_rows(column_panel, lax.all_gather(update, "col", axis=0, tiled=True))
    cross_block = -weighted * tile_mask
    update_panel = lax.all_gather(update, "row", axis=1, tiled=True)
    child_block = lax.psum_scatter(
        contract_rows(update_panel, weighted) + contract_rows(inverse, inverse_block),
        "col",
        scatter_dimension=0,
        tiled=True,
    )
    return (sigma_root, cross_block[None], child_block[None])


def solution(mesh):
    in_specs = (
        P(("depth", "row"), None),
        P("depth", "col", "row"),
        P("depth", "col", None),
        P("depth", "col"),
    )
    out_specs = (P(("depth", "row"), "col"), P("depth", "col", "row"), P("depth", "col", "row"))
    return jax.shard_map(shards, mesh=mesh, in_specs=in_specs, out_specs=out_specs, check_vma=False)
```

profile of v0, /device:TPU:0, one launch (start us, length us, event | category | flops | bytes accessed | tf_op | source)
XLA Modules:
  0.0 583.0 jit_solution(8713731432341738638)
XLA Ops:
  8.0 0.0 all-gather.6.cloned.1.call-start
  8.0 0.7 convert_bitcast_fusion
  8.7 0.1 broadcast_bitcast_fusion
  8.8 4.5 bitcast_multiply_fusion
  13.3 0.0 all-gather.6.cloned.1.call-update
  13.3 0.0 all-gather.12.cloned.1.call-start
  13.4 3.2 constant_dynamic-slice_fusion
  16.6 0.0 all-gather.12.cloned.1.call-update
  16.6 0.0 all-reduce.2.cloned.1.call-start
  16.6 31.7 %convolution_bitcast_fusion = f32[4096,1024]{0,1:T(8,128)} fusion(f32[512,4096]{1,0:T(8,128)} %param.4, s32[]{:T(128)S(6)} %select_n.9), kind=kOutput, calls=%fused_computation | convolution fusion | flops 25769803776 | bytes 27262980 | tf_op jit(solution)/shard_map/dot_general | solution.py:10
  48.3 0.0 all-reduce.2.cloned.1.call-update
  48.4 0.2 all-gather.8.cloned.1.call-start
  48.6 0.0 all-gather.6.cloned.1.call-done
  48.6 78.7 %all-gather.12.cloned.1.call-done = f32[1,2048,1024]{2,1,0:T(8,128)} async-done(((f32[1,512,1024]{2,1,0:T(8,128)}), f32[1,2048,1024]{2,1,0:T(8,128)}) %all-gather.12.cloned.1.call-update) | async-done | bytes 8388624 | tf_op jit(solution)/shard_map/all_gather | solution.py:41
  127.3 32.0 %fusion = f32[1024,1024]{1,0:T(8,128)} fusion(f32[1024,2048]{1,0:T(8,128)} %all-gather.6.cloned.1.call-done, f32[1,2048,1024]{2,1,0:T(8,128)} %all-gather.12.cloned.1.call-done), kind=kOutput, calls=%fused_computation.2 | convolution fusion | flops 25769803776 | bytes 20971520 | tf_op jit(solution)/shard_map/dot_general | solution.py:39
  159.3 0.0 all-gather.8.cloned.1.call-update
  159.3 0.0 all-gather.10.cloned.1.call-start
  159.4 0.5 all-gather.10.cloned.1.call-update
  159.9 0.3 reduce-scatter.2.cloned.1.call-start
  160.2 223.3 %all-reduce.2.cloned.1.call-done = f32[4096,1024]{0,1:T(8,128)} async-done(((f32[4096,1024]{0,1:T(8,128)}), f32[4096,1024]{0,1:T(8,128)}) %all-reduce.2.cloned.1.call-update) | async-done | bytes 16777232 | tf_op jit(solution)/shard_map/psum | solution.py:30
  383.5 0.0 all-gather.8.cloned.1.call-done
  383.5 59.3 %fusion.6 = f32[1024,1024]{1,0:T(8,128)} fusion(f32[4096,1024]{0,1:T(8,128)} %all-reduce.2.cloned.1.call-done, f32[4096,1024]{1,0:T(8,128)} %all-gather.8.cloned.1.call-done), kind=kOutput, calls=%fused_computation.14 | convolution fusion | flops 51539607552 | bytes 37748736 | tf_op jit(solution)/shard_map/dot_general | solution.py:10
  442.8 0.0 copy-start
  442.8 30.3 %fusion.7 = f32[2048,1024]{1,0:T(8,128)S(1)} fusion(f32[1024,2048]{1,0:T(8,128)} %all-gather.10.cloned.1.call-done, f32[1024,1024]{1,0:T(8,128)} %fusion.6), kind=kOutput, calls=%fused_computation.15 | convolution fusion | flops 25769803776 | bytes 20971520 | tf_op jit(solution)/shard_map/dot_general | solution.py:10
  473.1 0.0 copy-done
  473.2 0.0 copy-done.1
  473.2 16.0 %bitcast_add_fusion = f32[2048,1024]{1,0:T(8,128)} fusion(f32[2048,1024]{1,0:T(8,128)S(1)} %fusion.7, f32[1,512,2048]{2,1,0:T(8,128)S(1)} %copy-done.1, f32[1,512,1024]{2,1,0:T(8,128)S(1)} %copy-done), kind=kOutput, calls=%fused_computation.1 | convolution fusion | flops 12886999040 | bytes 23068672 | tf_op jit(solution)/shard_map/dot_general | solution.py:10
  489.2 0.0 reduce-scatter.2.cloned.1.call-update
  489.2 1.8 constant_dynamic-slice_fusion.1
  491.0 1.8 copy.8
  492.8 4.6 multiply_bitcast_fusion
  497.4 78.5 %reduce-scatter.2.cloned.1.call-done = f32[512,1024]{1,0:T(8,128)} async-done(((f32[2048,1024]{1,0:T(8,128)}), f32[512,1024]{1,0:T(8,128)}) %reduce-scatter.2.cloned.1.call-update) | async-done | bytes 2097168 | tf_op jit(solution)/shard_map/reduce_scatter | solution.py:48
  (2 shorter events, 0.0 us)
Async XLA Ops:
  8.0 40.6 %all-gather.6.cloned.1.call-start = ((), (), s32[]{:S(2)}) async-start(), calls=%async_computation.2 | async-start | bytes 12582912 | tf_op jit(solution)/shard_map/all_gather | solution.py:36
  13.3 113.9 %all-gather.12.cloned.1.call-start = ((), (), s32[]{:S(2)}) async-start(), calls=%async_computation.6 | async-start | bytes 10485760 | tf_op jit(solution)/shard_map/all_gather | solution.py:41
  16.6 367.0 %all-reduce.2.cloned.1.call-start = ((), (), s32[]{:S(2)}) async-start(), calls=%async_computation.1 | async-start | bytes 33554432 | tf_op jit(solution)/shard_map/psum | solution.py:30
  48.4 335.2 %all-gather.8.cloned.1.call-start = ((), (), s32[]{:S(2)}) async-start(), calls=%async_computation.3 | async-start | bytes 20971520 | tf_op jit(solution)/shard_map/all_gather | solution.py:45
  159.3 283.5 %all-gather.10.cloned.1.call-start = ((), (), s32[]{:S(2)}) async-start(), calls=%async_computation.4 | async-start | bytes 12582912 | tf_op jit(solution)/shard_map/all_gather | solution.py:47
  159.9 416.0 %reduce-scatter.2.cloned.1.call-start = ((), (), s32[]{:S(2)}) async-start(), calls=%async_computation.5 | async-start | bytes 10485760 | tf_op jit(solution)/shard_map/reduce_scatter | solution.py:48
  442.8 30.3 %copy-start = (f32[1,512,1024]{2,1,0:T(8,128)S(1)}, f32[1,512,1024]{2,1,0:T(8,128)}, u32[]{:S(2)}) copy-start(f32[1,512,1024]{2,1,0:T(8,128)} %constant_dynamic-slice_fusion) | copy-start | bytes 6291460
  442.8 30.3 %copy-start.1 = (f32[1,512,2048]{2,1,0:T(8,128)S(1)}, f32[1,512,2048]{2,1,0:T(8,128)}, u32[]{:S(2)}) copy-start(f32[1,512,2048]{2,1,0:T(8,128)} %param.6) | copy-start | bytes 12582916
Sparse Core Ops, SparseCore 0:
  13.5 22.5 all-gather.5
  38.5 88.7 all-gather.11
  159.5 157.4 all-gather.7
  319.0 19.9 all-gather.9
  489.3 86.5 reduce-scatter.1
Sparse Core Ops, SparseCore 1:
  48.4 335.0 all-reduce.1
where the time goes:
time: 583 us
  waiting for transfers between devices  381 us (65%)
  matrix products  169 us (29%)
  between operations  15.3 us (3%)
  other arithmetic  9.76 us (2%)
  local copies, waits for them, and re-layouts  6.83 us (1%)
    psum x1, waiting for transfers between devices, shards(): column_panel = lax.psum(term_value, ('depth', 'row'))  223 us
    dot_general x4, matrix products, contract_rows(): lax.dot_general(left, right, (((0,), (0,)), ((), ())), precision=lax.Prec...  137 us
    all_gather x1, waiting for transfers between devices, shards(): lax.all_gather(inverse_block, 'col', axis=0, tiled=True)  78.7 us
    reduce_scatter x1, waiting for transfers between devices, shards(): lax.psum_scatter(contract_rows(update_panel, weighted) + contract_rows(in...  78.5 us
    dot_general x1, matrix products, shards(): jnp.dot(factor_panel, lax.all_gather(inverse_block, 'col', axis=0, tiled=...  32 us
  transfers between devices with their start and end apart: 6, of which 3 were waited for; matrix products, arithmetic and copies ran while one was open for 23% of the time, Pallas kernels for 0%

commit v1 on v0

--- a/solution.py
+++ b/solution.py
@@ -4,6 +4,7 @@
 from jax.sharding import PartitionSpec as P
 
 TILE = 128
+PRECISION = lax.Precision.HIGH
 
 
 def contract_rows(left, right):
@@ -11,13 +12,12 @@
         left,
         right,
         (((0,), (0,)), ((), ())),
-        precision=lax.Precision.HIGHEST,
+        precision=PRECISION,
         preferred_element_type=jnp.float32,
     )
 
 
 def shards(linv_root, child_factor, child_inverse, structure):
-    highest = lax.Precision.HIGHEST
     n_col = lax.axis_size("col")
     n_row = lax.axis_size("row")
     col_at = lax.axis_index("col")
@@ -39,14 +39,15 @@
     update = jnp.dot(
         factor_panel,
         lax.all_gather(inverse_block, "col", axis=0, tiled=True),
-        precision=highest,
+        precision=PRECISION,
         preferred_element_type=jnp.float32,
     )
+    own_term, column_panel = lax.optimization_barrier((contract_rows(inverse, inverse_block), column_panel))
     weighted = contract_rows(column_panel, lax.all_gather(update, "col", axis=0, tiled=True))
     cross_block = -weighted * tile_mask
     update_panel = lax.all_gather(update, "row", axis=1, tiled=True)
     child_block = lax.psum_scatter(
-        contract_rows(update_panel, weighted) + contract_rows(inverse, inverse_block),
+        contract_rows(update_panel, weighted) + own_term,
         "col",
         scatter_dimension=0,
         tiled=True,

time: 583 us -> 522 us (0.90)
  matrix products: 169 us -> 103 us
    dot_general x4, matrix products: 137 us -> 83.7 us  [contract_rows(): lax.dot_general(left, right, (((0,), (0,)), ((), ())), precision=PRECISIO...]
    dot_general x1, matrix products: 32 us -> 19.5 us  [shards(): jnp.dot(factor_panel, lax.all_gather(inverse_block, 'col', axis=0, tiled=...]
    all_gather x1, waiting for transfers between devices: 78.7 us -> 90.6 us  [shards(): lax.all_gather(inverse_block, 'col', axis=0, tiled=True)]
    psum x1, waiting for transfers between devices: 223 us -> 213 us  [shards(): column_panel = lax.psum(term_value, ('depth', 'row'))]
  transfers between devices with their start and end apart: 6 -> 6, of which waited for: 3 -> 3; matrix products, arithmetic and copies ran while one was open for 23% -> 18% of each run, Pallas kernels for 0% -> 0%
where the time goes in v1:
time: 522 us
  waiting for transfers between devices  382 us (73%)
  matrix products  103 us (20%)
  between operations  15.3 us (3%)
  local copies, waits for them, and re-layouts  10.4 us (2%)
  other arithmetic  9.76 us (2%)
    psum x1, waiting for transfers between devices, shards(): column_panel = lax.psum(term_value, ('depth', 'row'))  213 us
    all_gather x1, waiting for transfers between devices, shards(): lax.all_gather(inverse_block, 'col', axis=0, tiled=True)  90.6 us
    dot_general x4, matrix products, contract_rows(): lax.dot_general(left, right, (((0,), (0,)), ((), ())), precision=PRECISIO...  83.7 us
    reduce_scatter x1, waiting for transfers between devices, shards(): lax.psum_scatter(contract_rows(update_panel, weighted) + own_term, 'col',...  78.5 us
    dot_general x1, matrix products, shards(): jnp.dot(factor_panel, lax.all_gather(inverse_block, 'col', axis=0, tiled=...  19.5 us
  transfers between devices with their start and end apart: 6, of which 3 were waited for; matrix products, arithmetic and copies ran while one was open for 18% of the time, Pallas kernels for 0%

profile of v1, /device:TPU:0, one launch (start us, length us, event | category | flops | bytes accessed | tf_op | source)
XLA Modules:
  0.0 521.5 jit_solution(18167949654860803445)
XLA Ops:
  8.0 0.0 all-gather.6.cloned.1.call-start
  8.0 0.7 convert_bitcast_fusion
  8.7 0.1 broadcast_bitcast_fusion
  8.8 4.5 bitcast_multiply_fusion
  13.3 0.0 all-gather.6.cloned.1.call-update
  13.3 0.0 all-gather.12.cloned.1.call-start
  13.4 3.2 constant_dynamic-slice_fusion
  16.6 0.0 all-gather.12.cloned.1.call-update
  16.6 0.0 all-reduce.2.cloned.1.call-start
  16.6 19.8 %convolution_bitcast_fusion = f32[4096,1024]{0,1:T(8,128)} fusion(f32[512,4096]{1,0:T(8,128)} %param.4, s32[]{:T(128)S(6)} %select_n.9), kind=kOutput, calls=%fused_computation | convolution fusion | flops 12884901888 | bytes 27262980 | tf_op jit(solution)/shard_map/dot_general | solution.py:11
  36.4 0.0 all-reduce.2.cloned.1.call-update
  36.4 0.2 all-gather.8.cloned.1.call-start
  36.7 0.0 all-gather.6.cloned.1.call-done
  36.7 90.6 %all-gather.12.cloned.1.call-done = f32[1,2048,1024]{2,1,0:T(8,128)} async-done(((f32[1,512,1024]{2,1,0:T(8,128)}), f32[1,2048,1024]{2,1,0:T(8,128)}) %all-gather.12.cloned.1.call-update) | async-done | bytes 8388624 | tf_op jit(solution)/shard_map/all_gather | solution.py:41
  127.3 19.5 %fusion = f32[1024,1024]{1,0:T(8,128)} fusion(f32[1024,2048]{1,0:T(8,128)} %all-gather.6.cloned.1.call-done, f32[1,2048,1024]{2,1,0:T(8,128)} %all-gather.12.cloned.1.call-done), kind=kOutput, calls=%fused_computation.1 | convolution fusion | flops 12884901888 | bytes 20971520 | tf_op jit(solution)/shard_map/dot_general | solution.py:39
  146.7 0.0 copy-start
  146.7 0.0 all-gather.8.cloned.1.call-update
  146.8 0.0 all-gather.10.cloned.1.call-start
  146.8 0.5 all-gather.10.cloned.1.call-update
  147.3 0.3 reduce-scatter.2.cloned.1.call-start
  147.6 0.7 copy-done
  148.3 10.9 %convolution_bitcast_fusion.1 = f32[2048,1024]{0,1:T(8,128)} fusion(f32[1,512,2048]{2,1,0:T(8,128)} %param.6, f32[1,512,1024]{2,1,0:T(8,128)S(1)} %copy-done), kind=kOutput, calls=%fused_computation.3 | convolution fusion | flops 6442450944 | bytes 14680064 | tf_op jit(solution)/shard_map/dot_general | solution.py:11
  159.2 212.7 %all-reduce.2.cloned.1.call-done = f32[4096,1024]{0,1:T(8,128)} async-done(((f32[4096,1024]{0,1:T(8,128)}), f32[4096,1024]{0,1:T(8,128)}) %all-reduce.2.cloned.1.call-update) | async-done | bytes 16777232 | tf_op jit(solution)/shard_map/psum | solution.py:30
  371.9 0.0 all-gather.8.cloned.1.call-done
  371.9 32.4 %fusion.6 = f32[1024,1024]{1,0:T(8,128)} fusion(f32[4096,1024]{0,1:T(8,128)} %all-reduce.2.cloned.1.call-done, f32[4096,1024]{1,0:T(8,128)} %all-gather.8.cloned.1.call-done), kind=kOutput, calls=%fused_computation.15 | convolution fusion | flops 25769803776 | bytes 37748736 | tf_op jit(solution)/shard_map/dot_general | solution.py:11
  404.3 20.6 %convolution_add_fusion = f32[2048,1024]{0,1:T(8,128)} fusion(f32[2048,1024]{0,1:T(8,128)} %convolution_bitcast_fusion.1, f32[1024,2048]{1,0:T(8,128)} %all-gather.10.cloned.1.call-done, f32[1024,1024]{1,0:T(8,128)} %fusion.6), kind=kOutput, calls=%fused_computation.7 | convolution fusion | flops 12886999040 | bytes 29360128 | tf_op jit(solution)/shard_map/dot_general | solution.py:11
  424.9 0.0 reduce-scatter.2.cloned.1.call-update
  424.9 1.8 constant_dynamic-slice_fusion.1
  426.7 1.8 copy.8
  428.5 4.6 multiply_bitcast_fusion
  433.1 78.5 %reduce-scatter.2.cloned.1.call-done = f32[512,1024]{0,1:T(8,128)} async-done(((f32[2048,1024]{0,1:T(8,128)}), f32[512,1024]{0,1:T(8,128)}) %reduce-scatter.2.cloned.1.call-update) | async-done | bytes 2097168 | tf_op jit(solution)/shard_map/reduce_scatter | solution.py:49
  511.5 2.9 copy.9
  (1 shorter events, 0.0 us)
Async XLA Ops:
  8.0 28.7 %all-gather.6.cloned.1.call-start = ((), (), s32[]{:S(2)}) async-start(), calls=%async_computation.2 | async-start | bytes 12582912 | tf_op jit(solution)/shard_map/all_gather | solution.py:36
  13.3 113.9 %all-gather.12.cloned.1.call-start = ((), (), s32[]{:S(2)}) async-start(), calls=%async_computation.6 | async-start | bytes 10485760 | tf_op jit(solution)/shard_map/all_gather | solution.py:41
  16.6 355.3 %all-reduce.2.cloned.1.call-start = ((), (), s32[]{:S(2)}) async-start(), calls=%async_computation.1 | async-start | bytes 33554432 | tf_op jit(solution)/shard_map/psum | solution.py:30
  36.4 335.4 %all-gather.8.cloned.1.call-start = ((), (), s32[]{:S(2)}) async-start(), calls=%async_computation.3 | async-start | bytes 20971520 | tf_op jit(solution)/shard_map/all_gather | solution.py:46
  146.7 1.6 copy-start
  146.8 257.5 %all-gather.10.cloned.1.call-start = ((), (), s32[]{:S(2)}) async-start(), calls=%async_computation.4 | async-start | bytes 12582912 | tf_op jit(solution)/shard_map/all_gather | solution.py:48
  147.3 364.2 %reduce-scatter.2.cloned.1.call-start = ((), (), s32[]{:S(2)}) async-start(), calls=%async_computation.5 | async-start | bytes 10485760 | tf_op jit(solution)/shard_map/reduce_scatter | solution.py:49
Sparse Core Ops, SparseCore 0:
  13.5 22.5 all-gather.5
  38.5 88.7 all-gather.11
  146.9 157.4 all-gather.7
  306.3 20.0 all-gather.9
  425.0 86.4 reduce-scatter.1
Sparse Core Ops, SparseCore 1:
  36.5 335.3 all-reduce.1

commit v2 on v1

--- a/solution.py
+++ b/solution.py
@@ -32,16 +32,16 @@
     factor = child_factor[0]
     inverse = child_inverse[0]
     tile_mask = jnp.repeat(structure[0], TILE).astype(jnp.float32)[:, None]
-    masked_factor = factor * tile_mask
-    factor_panel = lax.all_gather(masked_factor, "row", axis=1, tiled=True)
+    factor_panel = lax.all_gather(factor, "row", axis=1, tiled=True)
     nj_row = factor.shape[1]
     inverse_block = lax.dynamic_slice_in_dim(inverse, row_at * nj_row, nj_row, 1)
-    update = jnp.dot(
+    product = jnp.dot(
         factor_panel,
         lax.all_gather(inverse_block, "col", axis=0, tiled=True),
         precision=PRECISION,
         preferred_element_type=jnp.float32,
     )
+    update = jnp.where(tile_mask > 0, product, 0.0)
     own_term, column_panel = lax.optimization_barrier((contract_rows(inverse, inverse_block), column_panel))
     weighted = contract_rows(column_panel, lax.all_gather(update, "col", axis=0, tiled=True))
     cross_block = -weighted * tile_mask

time: 522 us -> 523 us (level)
  matrix products: 103 us -> 117 us
  waiting for transfers between devices: 382 us -> 369 us
    psum x1, waiting for transfers between devices: 213 us -> 198 us  [shards(): column_panel = lax.psum(term_value, ('depth', 'row'))]
    dot_general x1, matrix products: 19.5 us -> 32.8 us  [shards(): jnp.dot(factor_panel, lax.all_gather(inverse_block, 'col', axis=0, tiled=...]
  transfers between devices with their start and end apart: 6 -> 6, of which waited for: 3 -> 4; matrix products, arithmetic and copies ran while one was open for 18% -> 21% of each run, Pallas kernels for 0% -> 0%
where the time goes in v2:
time: 523 us; the launch traced here: 518 us
  waiting for transfers between devices  369 us (71%)
  matrix products  117 us (22%)
  between operations  15.7 us (3%)
  local copies, waits for them, and re-layouts  11.2 us (2%)
    psum x1, waiting for transfers between devices, shards(): column_panel = lax.psum(term_value, ('depth', 'row'))  198 us
    all_gather x1, waiting for transfers between devices, shards(): lax.all_gather(inverse_block, 'col', axis=0, tiled=True)  91.2 us
    dot_general x4, matrix products, contract_rows(): lax.dot_general(left, right, (((0,), (0,)), ((), ())), precision=PRECISIO...  83.7 us
    reduce_scatter x1, waiting for transfers between devices, shards(): lax.psum_scatter(contract_rows(update_panel, weighted) + own_term, 'col',...  78.4 us
    dot_general x1, matrix products, shards(): jnp.dot(factor_panel, lax.all_gather(inverse_block, 'col', axis=0, tiled=...  32.8 us
  transfers between devices with their start and end apart: 6, of which 4 were waited for; matrix products, arithmetic and copies ran while one was open for 21% of the time, Pallas kernels for 0%

profile of v2, /device:TPU:0, one launch (start us, length us, event | category | flops | bytes accessed | tf_op | source)
XLA Modules:
  0.0 517.6 jit_solution(1418949025297508497)
XLA Ops:
  8.0 0.0 all-gather.13.cloned.1.call-start
  8.0 0.7 all-gather.13.cloned.1.call-update
  8.7 0.0 all-gather.11.cloned.1.call-start
  8.8 3.2 constant_dynamic-slice_fusion
  11.9 0.0 all-gather.11.cloned.1.call-update
  12.0 0.0 all-reduce.2.cloned.1.call-start
  12.0 19.9 %convolution_bitcast_fusion = f32[4096,1024]{0,1:T(8,128)} fusion(f32[512,4096]{1,0:T(8,128)} %param.4, s32[]{:T(128)S(6)} %select_n.16), kind=kOutput, calls=%fused_computation | convolution fusion | flops 12884901888 | bytes 27262980 | tf_op jit(solution)/shard_map/dot_general | solution.py:11
  31.9 0.0 copy-start.1
  31.9 0.0 all-reduce.2.cloned.1.call-update
  31.9 0.0 all-gather.7.cloned.1.call-start
  32.0 0.6 copy-done.1
  32.5 0.1 bitcast_compare_fusion
  32.6 0.3 all-gather.13.cloned.1.call-done
  33.0 91.2 %all-gather.11.cloned.1.call-done = f32[1,2048,1024]{2,1,0:T(8,128)} async-done(((f32[1,512,1024]{2,1,0:T(8,128)}), f32[1,2048,1024]{2,1,0:T(8,128)}) %all-gather.11.cloned.1.call-update) | async-done | bytes 8388624 | tf_op jit(solution)/shard_map/all_gather | solution.py:40
  124.2 32.8 %select_bitcast_fusion = f32[1024,1024]{0,1:T(8,128)} fusion(pred[1024]{0:T(1024)(128)(4,1)S(1)} %bitcast_compare_fusion, f32[1,1024,2048]{2,1,0:T(8,128)} %all-gather.13.cloned.1.call-done, f32[1,2048,1024]{2,1,0:T(8,128)} %all-gather.11.cloned.1.call-done), kind=kOutput, calls=%fused_computation.7 | convolution fusion | flops 12885950464 | bytes 20972544 | tf_op jit(solution)/shard_map/dot_general | solution.py:38
  157.0 0.0 copy-start
  157.0 0.0 all-gather.7.cloned.1.call-update
  157.1 0.0 all-gather.9.cloned.1.call-start
  157.1 0.5 all-gather.9.cloned.1.call-update
  157.6 0.0 reduce-scatter.2.cloned.1.call-start
  157.7 0.9 copy-done
  158.6 10.8 %convolution_bitcast_fusion.1 = f32[2048,1024]{0,1:T(8,128)} fusion(f32[1,512,2048]{2,1,0:T(8,128)} %param.6, f32[1,512,1024]{2,1,0:T(8,128)S(1)} %copy-done), kind=kOutput, calls=%fused_computation.4 | convolution fusion | flops 6442450944 | bytes 14680064 | tf_op jit(solution)/shard_map/dot_general | solution.py:11
  169.4 198.0 %all-reduce.2.cloned.1.call-done = f32[4096,1024]{0,1:T(8,128)} async-done(((f32[4096,1024]{0,1:T(8,128)}), f32[4096,1024]{0,1:T(8,128)}) %all-reduce.2.cloned.1.call-update) | async-done | bytes 16777232 | tf_op jit(solution)/shard_map/psum | solution.py:30
  367.3 32.4 %fusion.11 = f32[1024,1024]{1,0:T(8,128)} fusion(f32[4096,1024]{0,1:T(8,128)} %all-reduce.2.cloned.1.call-done, f32[4096,1024]{0,1:T(8,128)} %all-gather.7.cloned.1.call-done), kind=kOutput, calls=%fused_computation.17 | convolution fusion | flops 25769803776 | bytes 37748736 | tf_op jit(solution)/shard_map/dot_general | solution.py:11
  399.8 20.6 %convolution_add_fusion = f32[2048,1024]{0,1:T(8,128)} fusion(f32[2048,1024]{0,1:T(8,128)} %convolution_bitcast_fusion.1, f32[1024,2048]{0,1:T(8,128)} %all-gather.9.cloned.1.call-done, f32[1024,1024]{1,0:T(8,128)} %fusion.11), kind=kOutput, calls=%fused_computation.8 | convolution fusion | flops 12886999040 | bytes 29360128 | tf_op jit(solution)/shard_map/dot_general | solution.py:11
  420.4 0.0 reduce-scatter.2.cloned.1.call-update
  420.5 0.1 broadcast_bitcast_fusion
  420.5 1.8 constant_dynamic-slice_fusion.1
  422.3 1.8 copy.8
  424.1 4.6 multiply_bitcast_fusion
  428.7 78.4 %reduce-scatter.2.cloned.1.call-done = f32[512,1024]{0,1:T(8,128)} async-done(((f32[2048,1024]{0,1:T(8,128)}), f32[512,1024]{0,1:T(8,128)}) %reduce-scatter.2.cloned.1.call-update) | async-done | bytes 2097168 | tf_op jit(solution)/shard_map/reduce_scatter | solution.py:49
  507.1 2.9 copy.9
  (3 shorter events, 0.0 us)
Async XLA Ops:
  8.0 25.0 %all-gather.13.cloned.1.call-start = ((), (), s32[]{:S(2)}) async-start(), calls=%async_computation.6 | async-start | bytes 12582912 | tf_op jit(solution)/shard_map/all_gather | solution.py:35
  8.7 115.5 %all-gather.11.cloned.1.call-start = ((), (), s32[]{:S(2)}) async-start(), calls=%async_computation.5 | async-start | bytes 10485760 | tf_op jit(solution)/shard_map/all_gather | solution.py:40
  12.0 355.4 %all-reduce.2.cloned.1.call-start = ((), (), s32[]{:S(2)}) async-start(), calls=%async_computation.1 | async-start | bytes 33554432 | tf_op jit(solution)/shard_map/psum | solution.py:30
  31.9 0.7 copy-start.1
  31.9 335.4 %all-gather.7.cloned.1.call-start = ((), (), s32[]{:S(2)}) async-start(), calls=%async_computation.2 | async-start | bytes 20971520 | tf_op jit(solution)/shard_map/all_gather | solution.py:46
  157.0 1.6 copy-start
  157.1 242.7 %all-gather.9.cloned.1.call-start = ((), (), s32[]{:S(2)}) async-start(), calls=%async_computation.3 | async-start | bytes 12582912 | tf_op jit(solution)/shard_map/all_gather | solution.py:48
  157.6 349.5 %reduce-scatter.2.cloned.1.call-start = ((), (), s32[]{:S(2)}) async-start(), calls=%async_computation.4 | async-start | bytes 10485760 | tf_op jit(solution)/shard_map/reduce_scatter | solution.py:49
Sparse Core Ops, SparseCore 0:
  10.4 22.5 all-gather.12
  35.4 88.7 all-gather.10
  157.2 157.4 all-gather.6
  316.6 20.0 all-gather.8
  420.6 86.4 reduce-scatter.1
Sparse Core Ops, SparseCore 1:
  32.0 335.3 all-reduce.1
